TPU v7x, 32 devices: a whole 2x2x4 slice. The times are simulated.
32 devices in a mesh: seq: 8 (over z, x), chan: 4 (over y, core).
Axes of the slice: x: 2, y: 2, z: 4, core: 2. Of those that a mesh axis runs over, the one named last changes fastest.
Arguments:
- token_ids: int32 [2048], P('seq'), may hold values from 0 to 511
- embed_table: bfloat16 [512, 8192], P(None, 'chan'), may hold values from -6 to 6
- se_query: bfloat16 [2048, 8192], P('seq', 'chan'), may hold values from -3 to 3
- se_key: bfloat16 [2048, 8192], P('seq', 'chan'), may hold values from -6 to 6
- se_filter: bfloat16 [512, 7], P('chan'), may hold values from -2 to 2
- mr_query: bfloat16 [2048, 8192], P('seq', 'chan'), may hold values from -3 to 3
- mr_key: bfloat16 [2048, 8192], P('seq', 'chan'), may hold values from -6 to 6
- mr_filter: bfloat16 [512, 128], P('chan'), may hold values from -0.5 to 0.5
- li_query: bfloat16 [2048, 8192], P('seq', 'chan'), may hold values from -3 to 3
- li_key: bfloat16 [2048, 8192], P('seq', 'chan'), may hold values from -6 to 6
- li_rate: float32 [512, 16], P('chan'), may hold values from 4.8828124e-06 to 0.05
- li_residue: float32 [512, 16], P('chan'), may hold values from -1.5 to 1.5
- attn_query: bfloat16 [2048, 8192], P('seq', 'chan'), may hold values from -7 to 7
- attn_key: bfloat16 [2048, 8192], P('seq', 'chan'), may hold values from -7 to 7
Outputs:
- block_out: bfloat16 [2048, 8192], P('seq', 'chan')
All inputs are finite; a program needn't handle non-finite values.
Results may differ from a plain program's by a relative error of at most 0.01.
Values may be sent and summed in bfloat16 or wider, within the bound.
A program may use at most 192 MiB of HBM per device.

v0:
```python
import jax
import jax.numpy as jnp
from jax import lax
from jax.sharding import PartitionSpec as P

HEAD_DIM = 128


HIGHEST = lax.Precision.HIGHEST


def from_behind(block, axis, distance):
    devices = range(lax.axis_size(axis))
    route = [(i - distance, i) for i in devices if i - distance in devices]
    return lax.ppermute(block, axis, route)


def carried_in(value, axis, combine, identity):
    count, here = (lax.axis_size(axis), lax.axis_index(axis))
    everything = jax.tree.map(lambda part: lax.all_gather(part, axis), value)
    start = jax.tree.map(
        lambda part, zero: jnp.broadcast_to(jnp.asarray(zero, part.dtype), part.shape),
        value,
        identity,
    )

    def step(k, before):
        reached = k < here
        new = combine(before, jax.tree.map(lambda part: part[k], everything))
        return jax.tree.map(lambda a, b: jnp.where(reached, a, b), new, before)

    return lax.fori_loop(0, count, step, start)


def toeplitz_tables(filters, taps):
    lag_grid = (
        jnp.arange(taps, dtype=jnp.int32)[:, None] - jnp.arange(taps, dtype=jnp.int32)[None, :]
    )
    tap_ids = jnp.arange(taps, dtype=jnp.int32)[:, None, None]
    near_select = (lag_grid[None] == tap_ids).astype(jnp.float32)
    far_select = ((lag_grid + taps)[None] == tap_ids).astype(jnp.float32)
    filters_f = filters.astype(jnp.float32)
    current = jnp.einsum("gk,kts->gts", filters_f, near_select, precision=HIGHEST)
    previous = jnp.einsum("gk,kts->gts", filters_f, far_select, precision=HIGHEST)
    return (current, previous)


def local(
    token_ids,
    embed_table,
    se_query,
    se_key,
    se_filter,
    mr_query,
    mr_key,
    mr_filter,
    li_query,
    li_key,
    li_rate,
    li_residue,
    attn_query,
    attn_key,
):
    f32 = jnp.float32
    bf16 = jnp.bfloat16
    row_count = token_ids.shape[0]
    channels = embed_table.shape[1]
    group_count = se_filter.shape[0]
    group_width = channels // group_count
    seq_count = lax.axis_size("seq")
    chan_count = lax.axis_size("chan")
    total_len = row_count * seq_count
    vocab_ids = jnp.arange(embed_table.shape[0], dtype=jnp.int32)
    one_hot = (token_ids[:, None] == vocab_ids[None, :]).astype(bf16)
    stream = jnp.dot(one_hot, embed_table, preferred_element_type=f32).astype(bf16)
    se_taps = se_filter.shape[1]
    se_input = (se_key.astype(f32) * stream.astype(f32)).astype(bf16)
    se_edge = from_behind(se_input[row_count - (se_taps - 1) :], "seq", 1)
    se_padded = jnp.concatenate([se_edge, se_input], 0)
    tap_weights = jnp.repeat(se_filter.astype(f32), group_width, axis=0)
    se_conv = jnp.zeros((row_count, channels), f32)
    for tap_index in range(se_taps):
        start_row = se_taps - 1 - tap_index
        se_conv = (
            se_conv
            + se_padded[start_row : start_row + row_count].astype(f32) * tap_weights[:, tap_index]
        )
    stream = (stream.astype(f32) + se_query.astype(f32) * se_conv).astype(bf16)
    mr_taps = mr_filter.shape[1]
    mr_input = (mr_key.astype(f32) * stream.astype(f32)).astype(bf16)
    mr_edge = from_behind(mr_input[row_count - (mr_taps - 1) :], "seq", 1)
    block_count = row_count // mr_taps
    extended = jnp.concatenate([jnp.zeros((1, channels), bf16), mr_edge, mr_input], 0)
    extended = extended.reshape(block_count + 1, mr_taps, group_count, group_width)
    current_f, previous_f = toeplitz_tables(mr_filter, mr_taps)
    current = current_f.astype(bf16)
    previous = previous_f.astype(bf16)
    mr_conv = jnp.einsum("gts,bsgc->btgc", current, extended[1:], preferred_element_type=f32)
    mr_conv = mr_conv + jnp.einsum(
        "gts,bsgc->btgc", previous, extended[:-1], preferred_element_type=f32
    )
    stream = (
        stream.astype(f32) + mr_query.astype(f32) * mr_conv.reshape(row_count, channels)
    ).astype(bf16)
    li_input = (li_key.astype(f32) * stream.astype(f32)).astype(bf16)
    gain = li_residue * jnp.sqrt(1.0 - jnp.exp(-2.0 * li_rate) + 1.0 / total_len)
    lag_values = jnp.arange(mr_taps, dtype=f32)
    kernel_rows = jnp.sum(gain[:, :, None] * jnp.exp(-li_rate[:, :, None] * lag_values), axis=1)
    intra, unused_far = toeplitz_tables(kernel_rows, mr_taps)
    blocks_f = li_input.astype(f32).reshape(block_count, mr_taps, group_count, group_width)
    local_conv = jnp.einsum("gts,bsgc->btgc", intra, blocks_f, precision=HIGHEST)
    to_end = jnp.exp(-li_rate[:, :, None] * (mr_taps - 1 - lag_values))
    block_states = jnp.einsum("gms,bsgc->bmgc", to_end, blocks_f, precision=HIGHEST)
    block_ids = jnp.arange(block_count, dtype=f32)
    tail_decay = jnp.exp(-li_rate[None] * (mr_taps * (block_count - 1 - block_ids))[:, None, None])
    shard_state = jnp.einsum("bgm,bmgc->mgc", tail_decay, block_states, precision=HIGHEST)
    rate_column = li_rate.T[:, :, None]
    shard_decay = jnp.exp(-rate_column * row_count)

    def combine(earlier, later):
        return (earlier[0] * later[0], earlier[1] * later[0] + later[1])

    prefix = carried_in(
        (shard_decay, shard_state),
        "seq",
        combine,
        (jnp.ones_like(shard_decay), jnp.zeros_like(shard_state)),
    )
    carry_in = prefix[1]
    block_lag = block_ids[:, None] - 1.0 - block_ids[None, :]
    mixing = jnp.exp(
        -li_rate[None, None] * (mr_taps * jnp.maximum(block_lag, 0.0))[:, :, None, None]
    )
    mixing = jnp.where(block_lag[:, :, None, None] >= 0, mixing, 0.0)
    lead_decay = jnp.exp(-li_rate[None] * (mr_taps * block_ids)[:, None, None])
    block_carry = jnp.einsum("bdgm,dmgc->bmgc", mixing, block_states, precision=HIGHEST)
    block_carry = block_carry + jnp.einsum("bgm,mgc->bmgc", lead_decay, carry_in, precision=HIGHEST)
    emit = gain[:, None, :] * jnp.exp(-li_rate[:, None, :] * (lag_values + 1.0)[None, :, None])
    carry_conv = jnp.einsum("gtm,bmgc->btgc", emit, block_carry, precision=HIGHEST)
    li_conv = (local_conv + carry_conv).reshape(row_count, channels)
    stream = (stream.astype(f32) + li_query.astype(f32) * li_conv).astype(bf16)
    head_dim = HEAD_DIM
    local_heads = channels // head_dim
    part_rows = row_count // chan_count
    chan_index = lax.axis_index("chan")
    queries = attn_query.reshape(row_count, local_heads, head_dim)
    keys_local = attn_key.reshape(row_count, local_heads, head_dim)
    values_local = stream.reshape(row_count, local_heads, head_dim)
    q_heads, k_heads, v_heads = (
        lax.all_to_all(
            lax.all_to_all(queries, "chan", split_axis=0, concat_axis=1, tiled=True),
            "seq",
            split_axis=1,
            concat_axis=0,
            tiled=True,
        ),
        lax.all_to_all(
            lax.all_to_all(keys_local, "chan", split_axis=0, concat_axis=1, tiled=True),
            "seq",
            split_axis=1,
            concat_axis=0,
            tiled=True,
        ),
        lax.all_to_all(
            lax.all_to_all(values_local, "chan", split_axis=0, concat_axis=1, tiled=True),
            "seq",
            split_axis=1,
            concat_axis=0,
            tiled=True,
        ),
    )
    k_all, v_all = (
        lax.all_gather(k_heads, "chan", axis=0, tiled=True),
        lax.all_gather(v_heads, "chan", axis=0, tiled=True),
    )
    key_index = jnp.arange(chan_count * seq_count * part_rows, dtype=jnp.int32)
    key_chan = key_index // (seq_count * part_rows)
    key_rest = key_index % (seq_count * part_rows)
    key_pos = key_rest // part_rows * row_count + key_chan * part_rows + key_rest % part_rows
    query_count = q_heads.shape[0]
    head_count = q_heads.shape[1]
    query_index = jnp.arange(query_count, dtype=jnp.int32)
    query_pos = (
        query_index // part_rows * row_count + chan_index * part_rows + query_index % part_rows
    )
    block_rows = 512
    scale = head_dim ** (-0.5)

    def attend_block(packed):
        query_block, pos_block = packed
        scores = jnp.einsum("qhd,khd->hqk", query_block, k_all, preferred_element_type=f32) * scale
        allowed = key_pos[None, :] <= pos_block[:, None]
        scores = jnp.where(allowed[None], scores, -1e30)
        peak = jnp.max(scores, axis=2, keepdims=True)
        weights = jnp.where(allowed[None], jnp.exp(scores - peak), 0.0)
        totals = jnp.sum(weights, axis=2)
        mixed = jnp.einsum("hqk,khd->qhd", weights.astype(bf16), v_all, preferred_element_type=f32)
        return (mixed / totals.T[:, :, None]).astype(bf16)

    attended = lax.map(
        attend_block,
        (
            q_heads.reshape(query_count // block_rows, block_rows, head_count, head_dim),
            query_pos.reshape(query_count // block_rows, block_rows),
        ),
    )
    attended = attended.reshape(query_count, head_count, head_dim)
    returned = lax.all_to_all(
        lax.all_to_all(attended, "seq", split_axis=0, concat_axis=1, tiled=True),
        "chan",
        split_axis=1,
        concat_axis=0,
        tiled=True,
    )
    return (stream.astype(f32) + returned.reshape(row_count, channels).astype(f32)).astype(bf16)


def solution(mesh):
    in_specs = (
        P("seq"),
        P(None, "chan"),
        P("seq", "chan"),
        P("seq", "chan"),
        P("chan", None),
        P("seq", "chan"),
        P("seq", "chan"),
        P("chan", None),
        P("seq", "chan"),
        P("seq", "chan"),
        P("chan", None),
        P("chan", None),
        P("seq", "chan"),
        P("seq", "chan"),
    )
    out_specs = P("seq", "chan")
    return jax.shard_map(local, mesh=mesh, in_specs=in_specs, out_specs=out_specs, check_vma=False)
```

profile of v0, /device:TPU:0, one launch (start us, length us, event | category | flops | bytes accessed | tf_op | source)
XLA Modules:
  0.0 410.7 jit_solution(9838245105805603530)
XLA Ops:
  6.5 2.6 copy.147
  9.2 4.2 %all-to-all-start.4 = ((bf16[256,16,128]{2,1,0:T(8,128)(2,1)}), bf16[256,16,128]{2,1,0:T(8,128)(2,1)}, u32[]{:S(2)}, u32[]{:S(2)}) async-start(bf16[256,16,128]{2,1,0:T(8,128)(2,1)} %bitcast.89), calls=%async_computation.4 | async-start | bytes 2097152 | tf_op jit(solution)/shard_map/all_to_all | solution.py:158
  13.5 3.0 fusion.23
  16.5 4.8 %collective-permute-start = (bf16[6,2048]{1,0:T(8,128)(2,1)S(1)}, bf16[6,2048]{1,0:T(8,128)(2,1)S(1)}, u32[]{:S(2)}, u32[]{:S(2)}) collective-permute-start(bf16[6,2048]{1,0:T(8,128)(2,1)S(1)} %slice.74), channel_id=1, source_target_pairs={{0,4},{4,8},{8,12},{12,16},{16,20},{20,24},{24,28},{1,5},{5,9},{9,... | collective-permute-start | bytes 73736 | tf_op jit(solution)/shard_map/ppermute | solution.py:15
  21.9 3.3 convert_bitcast_fusion.1
  25.2 1.7 multiply_exponential_fusion
  26.9 5.7 %convert_bitcast_fusion = bf16[128,128,128,1]{0,2,1,3:T(8,128)(2,1)} fusion(s32[128,128]{1,0:T(8,128)S(1)} %broadcast_add_fusion, bf16[128,128]{1,0:T(8,128)(2,1)S(1)} %copy-done.5), kind=kOutput, calls=%fused_computation.20 | convolution fusion | flops 541065216 | bytes 4292608 | tf_op jit(solution)/shard_map/gk,kts->gts/dot_general | solution.py:44
  32.8 6.7 %copy.128 = bf16[128,128,128,1]{2,1,3,0:T(8,128)(2,1)} copy(bf16[128,128,128,1]{0,2,1,3:T(8,128)(2,1)} %convert_bitcast_fusion) | data formatting | bytes 8388608 | tf_op jit(solution)/shard_map/convert_element_type | solution.py:97
  39.5 6.7 %copy.127 = bf16[128,128,128,1]{2,1,3,0:T(8,128)(2,1)} copy(bf16[128,128,128,1]{0,2,1,3:T(8,128)(2,1)} %convert_bitcast_fusion.1) | data formatting | bytes 8388608 | tf_op jit(solution)/shard_map/convert_element_type | solution.py:96
  46.3 4.4 %fusion.25 = (bf16[256,2048]{1,0:T(8,128)(2,1)S(1)}, bf16[256,2048]{1,0:T(8,128)(2,1)}) fusion(bf16[256,2048]{1,0:T(8,128)(2,1)} %param.22, f32[2048]{0:T(1024)S(1)} %bitcast.178, bf16[256,2048]{1,0:T(8,128)(2,1)S(1)} %get-tuple-element.165, bf16[6,2048]{1,0:T(8,128)(2,1)S(1)} %collective-permute-done, f32[2048]{0:T(1024)S(1)} %bitcast.179, ...), kind=kLoop, calls=%fused_computation.41 | loop fusion | flops 24641536 | bytes 6373376 | tf_op jit(solution)/shard_map/convert_element_type | solution.py:90
  51.6 4.4 %collective-permute-start.1 = (bf16[127,2048]{1,0:T(8,128)(2,1)}, bf16[127,2048]{1,0:T(8,128)(2,1)}, u32[]{:S(2)}, u32[]{:S(2)}) collective-permute-start(bf16[127,2048]{1,0:T(8,128)(2,1)} %slice.91), channel_id=1, source_target_pairs={{0,4},{4,8},{8,12},{12,16},{16,20},{20,24},{24,28},{1,5},{5,9},{9,... | collective-permute-start | bytes 1560584 | tf_op jit(solution)/shard_map/ppermute | solution.py:15
  56.8 5.8 %fusion.47 = f32[128,2,16,128]{3,2,1,0:T(8,128)} fusion(bf16[128,128,128,1]{2,1,3,0:T(8,128)(2,1)} %copy.127, bf16[2,128,128,16]{1,0,3,2:T(2,128)(2,1)S(1)} %slice.69), kind=kOutput, calls=%fused_computation.77 | convolution fusion | flops 134217728 | bytes 7340032 | tf_op jit(solution)/shard_map/gts,bsgc->btgc/dot_general | solution.py:98
  62.7 4.1 %collective-permute-done.1 = bf16[127,2048]{1,0:T(8,128)(2,1)} collective-permute-done((bf16[127,2048]{1,0:T(8,128)(2,1)}, bf16[127,2048]{1,0:T(8,128)(2,1)}, u32[]{:S(2)}, u32[]{:S(2)}) %collective-permute-start.1) | collective-permute-done | bytes 520224 | tf_op jit(solution)/shard_map/ppermute | solution.py:15
  70.9 4.5 %add_bitcast_fusion.2 = f32[2,128,128,16]{1,3,0,2:T(8,128)S(1)} fusion(f32[128,2,16,128]{3,2,1,0:T(8,128)S(1)} %copy-done.2, bf16[128,128,128,1]{2,1,3,0:T(8,128)(2,1)} %copy.128, bf16[2,128,128,16]{1,0,3,2:T(2,128)(2,1)S(1)} %slice.72), kind=kOutput, calls=%fused_computation.58 | convolution fusion | flops 134742016 | bytes 9437184 | tf_op jit(solution)/shard_map/gts,bsgc->btgc/dot_general | solution.py:99
  76.4 1.5 copy.168
  77.9 2.0 copy.94
  79.9 3.6 fusion.27
  83.5 1.5 copy.95
  85.3 2.5 convolution_bitcast_fusion
  87.8 4.6 %copy.101 = f32[2,16,128,16]{3,0,2,1:T(2,128)} copy(f32[2,16,128,16]{1,3,0,2:T(8,128)} %convolution_bitcast_fusion) | data formatting | bytes 524288 | tf_op jit(solution)/shard_map/gms,bsgc->bmgc/transpose | solution.py:113
  92.4 1.5 copy.117
  93.9 1.7 copy.118
  95.6 6.7 %all-to-all-start.5 = ((bf16[64,64,128]{2,0,1:T(8,128)(2,1)}), bf16[64,64,128]{2,0,1:T(8,128)(2,1)S(1)}, u32[]{:S(2)}, u32[]{:S(2)}) async-start(bf16[64,64,128]{2,0,1:T(8,128)(2,1)} %copy.118), calls=%async_computation.5 | async-start | bytes 2097152 | tf_op jit(solution)/shard_map/all_to_all | solution.py:157
  102.5 15.0 %fusion.104 = f32[16,128,1,16]{3,2,1,0:T(1,128)S(1)} fusion(f32[2,128,16,1]{0,3,1,2:T(1,128)} %bitcast.173, f32[2,16,128,16]{3,0,2,1:T(2,128)} %copy.101), kind=kOutput, calls=%fused_computation.160 | convolution fusion | flops 786432 | bytes 409600 | tf_op jit(solution)/shard_map/bgm,bmgc->mgc/dot_general | solution.py:116
  117.6 1.6 copy.132
  119.4 31.2 %all-gather = f32[128,128]{1,0:T(8,128)S(1)} all-gather(f32[16,128]{1,0:T(8,128)S(1)} %get-tuple-element.161), channel_id=2, replica_groups=mesh['seq'=8,'chan'=4] {'seq'}, dimensions={0}, use_global_device_ids=true | all-gather | bytes 73728 | tf_op jit(solution)/shard_map/all_gather | solution.py:20
  151.2 6.1 %fusion.20 = f32[128,128,128,1]{2,0,1,3:T(8,128)} fusion(s32[128,128]{1,0:T(8,128)S(1)} %iota_subtract_fusion, f32[128,128]{1,0:T(8,128)S(1)} %multiply_reduce_fusion), kind=kOutput, calls=%fused_computation.26 | convolution fusion | flops 3223322624 | bytes 8519680 | tf_op jit(solution)/shard_map/gk,kts->gts/dot_general | solution.py:43
  159.0 2.2 all-gather.10.cloned.1.call-done
  161.2 8.3 %while.18 = (s32[]{:T(128)}, f32[16,128,16]{1,2,0:T(8,128)S(1)}, s32[]{:T(128)}, f32[8,16,128,1]{2,1,3,0:T(8,128)S(1)}, f32[8,16,128,16]{2,3,1,0:T(8,128)}, /*index=5*/s32[]{:T(128)}, s32[]{:T(128)}) while((s32[]{:T(128)}, f32[16,128,16]{1,2,0:T(8,128)S(1)}, s32[]{:T(128)}, f32[8,16,128,1]{2,1,3,0:T(8,128)S(1)}, ...), condition=%wide.region_2.3_spmd.clone, body=%wide.region_1.2_spmd.clone.sunk | while | flops 131076 | bytes 417905 | solution.py:32
  169.9 17.5 %add_bitcast_fusion.1 = f32[2,16,128,16]{3,0,2,1:T(2,128)S(1)} fusion(f32[2,16,128,16]{3,0,2,1:T(2,128)} %copy.101, pred[2,2]{1,0:T(4,128)(4,1)S(1)} %fusion.96, f32[16,128,2]{2,1,0:T(8,128)} %get-tuple-element.164, f32[16,128,16]{2,1,0:T(8,128)S(1)} %copy.102, f32[2,2]{1,0:T(2,128)S(1)} %maximum_multiply_fusion, f32[128,16]{0,1:T(8,128)S(1)} %get-tuple-element.162), kind=kOutput, calls=%fused_computation.56 | convolution fusion | flops 1720320 | bytes 679956 | tf_op jit(solution)/shard_map/bdgm,dmgc->bmgc/dot_general | solution.py:136
  187.4 4.9 %fusion.31 = f32[128,2,16,128]{3,2,1,0:T(8,128)S(1)} fusion(f32[2,16,128,16]{3,0,2,1:T(2,128)S(1)} %add_bitcast_fusion.1, f32[128]{0:T(128)S(1)} %iota_add_fusion, f32[128,16]{1,0:T(8,128)S(1)} %copy.97, f32[128,16]{1,0:T(8,128)S(1)} %copy.96), kind=kOutput, calls=%fused_computation.52 | convolution fusion | flops 101187584 | bytes 2376192 | tf_op jit(solution)/shard_map/gtm,bmgc->btgc/dot_general | solution.py:139
  192.3 14.3 %add_bitcast_fusion = f32[2,128,128,16]{1,3,0,2:T(8,128)S(1)} fusion(f32[128,2,16,128]{3,2,1,0:T(8,128)S(1)} %fusion.31, f32[128,128,128,1]{2,0,1,3:T(8,128)} %fusion.20, bf16[2,128,128,16]{1,0,3,2:T(2,128)(2,1)S(1)} %reshape.228), kind=kOutput, calls=%fused_computation.55 | convolution fusion | flops 805830656 | bytes 13631488 | tf_op jit(solution)/shard_map/gts,bsgc->btgc/dot_general | solution.py:111
  207.7 1.5 copy.167
  209.2 1.9 copy.107
  211.2 2.0 fusion.28
  213.4 16.9 %all_to_all.132 = bf16[256,16,128]{2,1,0:T(8,128)(2,1)S(1)} all-to-all(bf16[256,16,128]{2,1,0:T(8,128)(2,1)S(1)} %bitcast.168), channel_id=1, replica_groups=mesh['seq'=8,'chan'=4] {'chan'}, dimensions={0} | all-to-all | bytes 2097152 | tf_op jit(solution)/shard_map/all_to_all | solution.py:165
  231.3 28.7 %all_to_all.133 = bf16[64,64,128]{2,0,1:T(8,128)(2,1)S(1)} all-to-all(bf16[64,64,128]{2,0,1:T(8,128)(2,1)S(1)} %copy.109), channel_id=1, replica_groups=mesh['seq'=8,'chan'=4] {'seq'}, dimensions={1} | all-to-all | bytes 2097152 | tf_op jit(solution)/shard_map/all_to_all | solution.py:164
  260.7 1.5 copy.112
  262.2 1.5 copy.146
  263.6 26.8 %all_to_all.134 = bf16[256,16,128]{2,1,0:T(8,128)(2,1)S(1)} all-to-all(bf16[256,16,128]{2,1,0:T(8,128)(2,1)S(1)} %bitcast.169), channel_id=1, replica_groups=mesh['seq'=8,'chan'=4] {'chan'}, dimensions={0} | all-to-all | bytes 2097152 | tf_op jit(solution)/shard_map/all_to_all | solution.py:151
  290.7 1.7 copy.114
  292.4 3.8 all-to-all-start.3
  296.9 24.8 %all-to-all-done.3 = bf16[64,64,128]{2,0,1:T(8,128)(2,1)S(1)} async-done(((bf16[64,64,128]{2,0,1:T(8,128)(2,1)}), bf16[64,64,128]{2,0,1:T(8,128)(2,1)S(1)}, u32[]{:S(2)}, u32[]{:S(2)}) %all-to-all-start.3) | async-done | bytes 1048608 | tf_op jit(solution)/shard_map/all_to_all | solution.py:150
  322.8 20.0 %fusion.103 = (f32[8,512]{1,0:T(8,128)S(1)}, bf16[8,512,2048]{2,1,0:T(8,128)(2,1)}) fusion(pred[512,2048]{1,0:T(8,128)(4,1)S(1)} %broadcast_compare_fusion, bf16[512,8,128]{2,0,1:T(8,128)(2,1)} %bitcast.172, bf16[2048,8,128]{2,0,1:T(8,128)(2,1)} %all-gather.8.cloned.1.call-done), kind=kOutput, calls=%fused_computation.159 | convolution fusion | flops 2197817344 | bytes 23085056 | tf_op jit(solution)/shard_map/while/body/eval_jaxpr/sub | solution.py:195
  342.8 10.5 %fusion.30 = bf16[512,8,128]{0,2,1:T(8,128)(2,1)S(1)} fusion(bf16[2048,8,128]{0,2,1:T(8,128)(2,1)} %all-gather.6.cloned.1.call-done, bf16[8,512,2048]{2,1,0:T(8,128)(2,1)} %get-tuple-element.168, f32[512,8]{0,1:T(8,128)S(1)} %bitcast.184), kind=kOutput, calls=%fused_computation.51 | convolution fusion | flops 2148532224 | bytes 22036480 | tf_op jit(solution)/shard_map/while/body/eval_jaxpr/hqk,khd->qhd/dot_general | solution.py:197
  354.1 29.1 %all_to_all.135 = bf16[512,8,128]{2,1,0:T(8,128)(2,1)S(1)} all-to-all(bf16[512,8,128]{2,1,0:T(8,128)(2,1)S(1)} %copy.121), channel_id=1, replica_groups=mesh['seq'=8,'chan'=4] {'seq'}, dimensions={0} | all-to-all | bytes 2097152 | tf_op jit(solution)/shard_map/all_to_all | solution.py:209
  384.2 16.9 %all_to_all.136 = bf16[64,64,128]{2,0,1:T(8,128)(2,1)S(1)} all-to-all(bf16[64,64,128]{2,0,1:T(8,128)(2,1)S(1)} %copy.123), channel_id=1, replica_groups=mesh['seq'=8,'chan'=4] {'chan'}, dimensions={1} | all-to-all | bytes 2097152 | tf_op jit(solution)/shard_map/all_to_all | solution.py:208
  402.2 1.7 fusion.29
  (95 shorter events, 27.0 us)
Async XLA Ops:
  6.5 6.9 %copy-start = (bf16[512,2048]{1,0:T(8,128)(2,1)S(1)}, bf16[512,2048]{1,0:T(8,128)(2,1)}, u32[]{:S(2)}) copy-start(bf16[512,2048]{1,0:T(8,128)(2,1)} %param.17) | copy-start | bytes 6291460
  6.5 6.9 %copy-start.10 = (s32[256]{0:T(256)S(1)}, s32[256]{0:T(256)}, u32[]{:S(2)}) copy-start(s32[256]{0:T(256)} %param.16) | copy-start | bytes 3076
  9.2 83.2 %all-to-all-start.4 = ((bf16[256,16,128]{2,1,0:T(8,128)(2,1)}), bf16[256,16,128]{2,1,0:T(8,128)(2,1)}, u32[]{:S(2)}, u32[]{:S(2)}) async-start(bf16[256,16,128]{2,1,0:T(8,128)(2,1)} %bitcast.89), calls=%async_computation.4 | async-start | bytes 2097152 | tf_op jit(solution)/shard_map/all_to_all | solution.py:158
  13.4 7.9 %copy-start.8 = (bf16[128,7]{0,1:T(8,128)(2,1)S(1)}, bf16[128,7]{0,1:T(8,128)(2,1)}, u32[]{:S(2)}) copy-start(bf16[128,7]{0,1:T(8,128)(2,1)} %param.20) | copy-start | bytes 5380
  13.4 8.4 %copy-start.6 = (f32[128,16]{0,1:T(8,128)S(1)}, f32[128,16]{0,1:T(8,128)}, u32[]{:S(2)}) copy-start(f32[128,16]{0,1:T(8,128)} %param.27) | copy-start | bytes 24580
  13.5 8.4 %copy-start.7 = (f32[128,16]{0,1:T(8,128)S(1)}, f32[128,16]{0,1:T(8,128)}, u32[]{:S(2)}) copy-start(f32[128,16]{0,1:T(8,128)} %param.26) | copy-start | bytes 24580
  13.5 8.4 %copy-start.5 = (bf16[128,128]{1,0:T(8,128)(2,1)S(1)}, bf16[128,128]{1,0:T(8,128)(2,1)}, u32[]{:S(2)}) copy-start(bf16[128,128]{1,0:T(8,128)(2,1)} %param.23) | copy-start | bytes 98308
  16.5 29.8 %collective-permute-start = (bf16[6,2048]{1,0:T(8,128)(2,1)S(1)}, bf16[6,2048]{1,0:T(8,128)(2,1)S(1)}, u32[]{:S(2)}, u32[]{:S(2)}) collective-permute-start(bf16[6,2048]{1,0:T(8,128)(2,1)S(1)} %slice.74), channel_id=1, source_target_pairs={{0,4},{4,8},{8,12},{12,16},{16,20},{20,24},{24,28},{1,5},{5,9},{9,... | collective-permute-start | bytes 73736 | tf_op jit(solution)/shard_map/ppermute | solution.py:15
  32.8 6.7 %copy-start.9 = (bf16[384]{0:T(512)(128)(2,1)}, bf16[384]{0:T(512)(128)(2,1)S(1)}, u32[]{:S(2)}) copy-start(bf16[384]{0:T(512)(128)(2,1)S(1)} %pad.clone) | copy-start | bytes 2308
  39.5 6.8 %copy-start.4 = (bf16[256,2048]{1,0:T(8,128)(2,1)S(1)}, bf16[256,2048]{1,0:T(8,128)(2,1)}, u32[]{:S(2)}) copy-start(bf16[256,2048]{1,0:T(8,128)(2,1)} %get-tuple-element.166) | copy-start | bytes 3145732
  51.6 15.3 %collective-permute-start.1 = (bf16[127,2048]{1,0:T(8,128)(2,1)}, bf16[127,2048]{1,0:T(8,128)(2,1)}, u32[]{:S(2)}, u32[]{:S(2)}) collective-permute-start(bf16[127,2048]{1,0:T(8,128)(2,1)} %slice.91), channel_id=1, source_target_pairs={{0,4},{4,8},{8,12},{12,16},{16,20},{20,24},{24,28},{1,5},{5,9},{9,... | collective-permute-start | bytes 1560584 | tf_op jit(solution)/shard_map/ppermute | solution.py:15
  56.8 10.0 %slice-start = ((bf16[384]{0:T(512)(128)(2,1)}), bf16[256]{0:T(256)(128)(2,1)S(1)}, s32[]{:S(2)}) async-start(bf16[384]{0:T(512)(128)(2,1)} %copy-done.9), calls=%async_computation.11 | async-start | bytes 1024 | tf_op jit(solution)/shard_map/slice | solution.py:100
  68.2 2.7 copy-start.2
  77.9 2.0 copy-start.3
  95.6 61.9 %all-to-all-start.5 = ((bf16[64,64,128]{2,0,1:T(8,128)(2,1)}), bf16[64,64,128]{2,0,1:T(8,128)(2,1)S(1)}, u32[]{:S(2)}, u32[]{:S(2)}) async-start(bf16[64,64,128]{2,0,1:T(8,128)(2,1)} %copy.118), calls=%async_computation.5 | async-start | bytes 2097152 | tf_op jit(solution)/shard_map/all_to_all | solution.py:157
  102.3 58.9 %all-gather.10.cloned.1.call-start = ((), (), s32[]{:S(2)}) async-start(), calls=%async_computation.10 | async-start | bytes 1179648 | tf_op jit(solution)/shard_map/all_gather | solution.py:20
  119.2 203.6 %all-gather.8.cloned.1.call-start = ((), (), s32[]{:S(2)}) async-start(), calls=%async_computation.9 | async-start | bytes 5242880 | tf_op jit(solution)/shard_map/all_gather | solution.py:173
  158.6 184.2 %all-gather.6.cloned.1.call-start = ((), (), s32[]{:S(2)}) async-start(), calls=%async_computation.8 | async-start | bytes 5242880 | tf_op jit(solution)/shard_map/all_gather | solution.py:174
  292.4 29.2 %all-to-all-start.3 = ((bf16[64,64,128]{2,0,1:T(8,128)(2,1)}), bf16[64,64,128]{2,0,1:T(8,128)(2,1)S(1)}, u32[]{:S(2)}, u32[]{:S(2)}) async-start(bf16[64,64,128]{2,0,1:T(8,128)(2,1)} %copy.114), calls=%async_computation.3 | async-start | bytes 2097152 | tf_op jit(solution)/shard_map/all_to_all | solution.py:150
  402.2 1.8 copy-start.1
Sparse Core Ops, SparseCore 0:
  119.3 41.8 all-gather.9
  162.8 33.2 all-gather.7
  262.3 42.2 all-gather.5
where the time goes:
time: 417 us; the launch traced here: 411 us
  blocking collectives  150 us (36%)
  matrix products  113 us (27%)
  local copies, waits for them, and re-layouts  53.5 us (13%)
  waiting for transfers between devices  31.1 us (7%)
  starting transfers between devices  24.7 us (6%)
  other arithmetic  24.6 us (6%)
  between operations  13.8 us (3%)
    all_gather x1, blocking collectives, carried_in(): everything = jax.tree.map(lambda part: lax.all_gather(part, axis), value)  31.2 us
    all_to_all x1, blocking collectives, local(): lax.all_to_all(attended, 'seq', split_axis=0, concat_axis=1, tiled=True)  29.1 us
    all_to_all x1, blocking collectives, local(): lax.all_to_all(lax.all_to_all(values_local, 'chan', split_axis=0, concat_...  28.7 us
    all_to_all x1, blocking collectives, local(): lax.all_to_all(queries, 'chan', split_axis=0, concat_axis=1, tiled=True)  26.8 us
    all_to_all x1, waiting for transfers between devices, local(): lax.all_to_all(lax.all_to_all(queries, 'chan', split_axis=0, concat_axis=...  24.8 us
    sub x1, matrix products, attend_block(): weights = jnp.where(allowed[None], jnp.exp(scores - peak), 0.0)  20 us
    dot_general x1, matrix products, local(): jnp.einsum('bdgm,dmgc->bmgc', mixing, block_states, precision=HIGHEST)  17.5 us
    all_to_all x1, blocking collectives, local(): lax.all_to_all(values_local, 'chan', split_axis=0, concat_axis=1, tiled=T...  16.9 us
  transfers between devices with their start and end apart: 8, of which 3 were waited for; matrix products, arithmetic and copies ran while one was open for 41% of the time, Pallas kernels for 0%

commit v1 on v0

--- a/solution.py
+++ b/solution.py
@@ -1,6 +1,9 @@
+import functools
 import jax
 import jax.numpy as jnp
 from jax import lax
+from jax.experimental import pallas as pl
+from jax.experimental.pallas import tpu as pltpu
 from jax.sharding import PartitionSpec as P
 
 HEAD_DIM = 128
@@ -215,6 +218,423 @@
     return (stream.astype(f32) + returned.reshape(row_count, channels).astype(f32)).astype(bf16)
 
 
+LANES = 128
+HALO = 16
+MESH = pl.DeviceIdType.MESH
+
+
+def fused(
+    n, total_len,
+    ids_ref, table_ref, sq_ref, sk_ref, sw_ref, mq_ref, mk_ref, mf_ref, lq_ref, lk_ref,
+    rate_ref, res_ref, q_hbm, k_hbm, out_hbm,
+    st, xs, hs, hx, mx, lx, lc, wt, s_mine, s_all, qh, kh, vh, ob, vb,
+    qss, qrs, kss, krs, vss, vrs, oss, ors, hss, hrs, sss, srs, own,
+):
+    f32, bf16 = jnp.float32, jnp.bfloat16
+    me = lax.axis_index("seq")
+    rows, chans = sq_ref.shape
+    tiles = chans // LANES
+    width = chans // n
+    per = width // LANES
+    half = rows // 2
+    groups = mf_ref.shape[0]
+    gpt = groups // tiles
+    gw = LANES // gpt
+    modes = LANES // gpt
+    taps = sw_ref.shape[0]
+
+    def lanes(start, size):
+        return pl.ds(pl.multiple_of(start, LANES), size)
+
+    def block(i):
+        return pl.ds(pl.multiple_of(i * rows, rows), rows)
+
+    barrier = pltpu.get_barrier_semaphore()
+
+    def greet(i, c):
+        pl.semaphore_signal(
+            barrier, inc=1, device_id={"seq": lax.rem(me + i, n)}, device_id_type=MESH
+        )
+        return c
+
+    lax.fori_loop(1, n, greet, 0)
+    pl.semaphore_wait(barrier, n - 1)
+
+    def spread(src, dst, ss, rs, peer, owner):
+        return pltpu.make_async_remote_copy(
+            src_ref=src.at[:, lanes(peer * width, width)],
+            dst_ref=dst.at[block(owner), :],
+            send_sem=ss.at[peer], recv_sem=rs.at[owner],
+            device_id={"seq": peer}, device_id_type=MESH,
+        )
+
+    def give_back(peer, owner):
+        return pltpu.make_async_remote_copy(
+            src_ref=ob.at[block(peer), :],
+            dst_ref=out_hbm.at[:, lanes(owner * width, width)],
+            send_sem=oss.at[peer], recv_sem=ors.at[owner],
+            device_id={"seq": peer}, device_id_type=MESH,
+        )
+
+    def state_copy(peer, owner):
+        return pltpu.make_async_remote_copy(
+            src_ref=s_mine, dst_ref=s_all.at[owner],
+            send_sem=sss.at[peer], recv_sem=srs.at[owner],
+            device_id={"seq": peer}, device_id_type=MESH,
+        )
+
+    nxt = lax.rem(me + 1, n)
+    se_halo = pltpu.make_async_remote_copy(
+        src_ref=hs, dst_ref=hx, send_sem=hss.at[0], recv_sem=hrs.at[0],
+        device_id={"seq": nxt}, device_id_type=MESH,
+    )
+    mr_halo = pltpu.make_async_remote_copy(
+        src_ref=mx.at[pl.ds(rows, half), :], dst_ref=mx.at[pl.ds(0, half), :],
+        send_sem=hss.at[1], recv_sem=hrs.at[1],
+        device_id={"seq": nxt}, device_id_type=MESH,
+    )
+
+    def send_all(src, dst, ss, rs):
+        def one(i, c):
+            spread(src, dst, ss, rs, lax.rem(me + i, n), me).start()
+            return c
+
+        lax.fori_loop(1, n, one, 0)
+
+    own_q = pltpu.make_async_copy(q_hbm.at[:, lanes(me * width, width)], qh.at[block(me), :], own.at[0])
+    own_k = pltpu.make_async_copy(k_hbm.at[:, lanes(me * width, width)], kh.at[block(me), :], own.at[1])
+    own_q.start()
+    own_k.start()
+
+    def iota(shape, dim):
+        return lax.broadcasted_iota(jnp.int32, shape, dim)
+
+    vocab = table_ref.shape[0]
+    ids_row = jnp.broadcast_to(ids_ref[...], (rows, rows))
+    eye = iota((rows, rows), 0) == iota((rows, rows), 1)
+    ids_col = jnp.sum(jnp.where(eye, ids_row, 0.0), axis=1, keepdims=True).astype(jnp.int32)
+    one_hot = (iota((rows, vocab), 1) == ids_col).astype(f32).astype(bf16)
+
+    def embed(j, c):
+        at = lanes(j * 2 * LANES, 2 * LANES)
+        e = jnp.dot(one_hot, table_ref[:, at], preferred_element_type=f32)
+        st[:, at] = e.astype(bf16)
+        gated = (sk_ref[:, at].astype(f32) * e).astype(bf16)
+        xs[pl.ds(HALO, rows), at] = gated.astype(f32)
+        hs[:, at] = gated[rows - HALO :, :]
+        return c
+
+    lax.fori_loop(0, tiles // 2, embed, 0)
+
+    @pl.when(me < n - 1)
+    def _():
+        se_halo.start()
+
+    send_all(q_hbm, qh, qss, qrs)
+
+    @pl.when(me > 0)
+    def _():
+        se_halo.wait_recv()
+
+    @pl.when(me == 0)
+    def _():
+        hx[...] = jnp.zeros_like(hx)
+        mx[pl.ds(0, half), :] = jnp.zeros((half, chans), bf16)
+
+    def short(j, c):
+        at = lanes(j * LANES, LANES)
+        xs[pl.ds(0, HALO), at] = hx[:, at].astype(f32)
+        conv = jnp.zeros((rows, LANES), f32)
+        for k in range(taps):
+            conv = conv + xs[pl.ds(HALO - k, rows), at] * sw_ref[pl.ds(k, 1), at]
+        s1 = (st[:, at].astype(f32) + sq_ref[:, at].astype(f32) * conv).astype(bf16)
+        st[:, at] = s1
+        mx[pl.ds(half, rows), at] = (mk_ref[:, at].astype(f32) * s1.astype(f32)).astype(bf16)
+        return c
+
+    lax.fori_loop(0, tiles, short, 0)
+
+    @pl.when(me < n - 1)
+    def _():
+        mr_halo.start()
+
+    send_all(k_hbm, kh, kss, krs)
+
+    @pl.when(me > 0)
+    def _():
+        mr_halo.wait_recv()
+
+    eye_l = iota((LANES, LANES), 0) == iota((LANES, LANES), 1)
+    lane_group = iota((half, 2 * LANES), 1) % LANES // gw
+    back = (rows - 1 - iota((LANES, rows), 1)).astype(f32)
+    causal = iota((half, rows), 1) <= iota((half, rows), 0) + half
+
+    def column(row):
+        return jnp.sum(
+            jnp.where(eye_l, jnp.broadcast_to(row, (LANES, LANES)), 0.0), axis=1, keepdims=True
+        )
+
+    def gain_of(j):
+        rate = rate_ref[pl.ds(j, 1), :]
+        return rate, res_ref[pl.ds(j, 1), :] * jnp.sqrt(
+            1.0 - jnp.exp(-2.0 * rate) + 1.0 / total_len
+        )
+
+    def pick(values, height, lg):
+        acc = values[0:height, :]
+        for g in range(1, gpt):
+            acc = jnp.where(lg == g, values[g * height : (g + 1) * height, :], acc)
+        return acc
+
+    def toeplitz(kernels, mask):
+        for g in range(gpt):
+            wide = jnp.broadcast_to(kernels[g : g + 1, :], (half, rows))
+            rolled = pltpu.roll(wide, half + 1, 1, stride=1, stride_axis=0)
+            if mask is not None:
+                rolled = jnp.where(mask, rolled, 0.0)
+            wt[pl.ds(g * half, half), :] = rolled.astype(bf16)
+
+    def stack(acc):
+        return jnp.concatenate([acc[:, :LANES], acc[:, LANES:]], axis=0)
+
+    lane_group_m = iota((modes, LANES), 1) // gw
+
+    def medium(j, c):
+        at = lanes(j * LANES, LANES)
+        toeplitz(mf_ref[pl.ds(pl.multiple_of(j * gpt, gpt), gpt), :], None)
+        both = jnp.concatenate([mx[pl.ds(0, rows), at], mx[pl.ds(half, rows), at]], axis=1)
+        conv = stack(
+            pick(jnp.dot(wt[...], both, preferred_element_type=f32), half, lane_group)
+        )
+        s2 = (st[:, at].astype(f32) + mq_ref[:, at].astype(f32) * conv).astype(bf16)
+        st[:, at] = s2
+        gated = (lk_ref[:, at].astype(f32) * s2.astype(f32)).astype(bf16)
+        lx[:, at] = gated
+        fade = jnp.exp(-column(rate_ref[pl.ds(j, 1), :]) * back).astype(bf16)
+        ends = jnp.dot(fade, gated, preferred_element_type=f32)
+        s_mine[:, at] = pick(ends, modes, lane_group_m).astype(bf16)
+        return c
+
+    lax.fori_loop(0, tiles, medium, 0)
+
+    def push_state(p, c):
+        state_copy(p, me).start()
+        return c
+
+    lax.fori_loop(me + 1, n, push_state, 0)
+
+    def long_local(j, c):
+        at = lanes(j * LANES, LANES)
+        rate, gain = gain_of(j)
+        fade = jnp.exp(-column(rate) * back) * column(gain)
+        toeplitz(jnp.sum(fade.reshape(gpt, modes, rows), axis=1), causal)
+        x = lx[:, at]
+        first = jnp.concatenate([jnp.zeros((half, LANES), bf16), x[:half, :]], axis=0)
+        both = jnp.concatenate([first, x], axis=1)
+        lc[:, at] = stack(
+            pick(jnp.dot(wt[...], both, preferred_element_type=f32), half, lane_group)
+        )
+        return c
+
+    lax.fori_loop(0, tiles, long_local, 0)
+
+    def take_state(p, c):
+        state_copy(me, p).wait_recv()
+        return c
+
+    lax.fori_loop(0, me, take_state, 0)
+
+    after = (iota((rows, LANES), 0) + 1).astype(f32)
+    same = iota((LANES, LANES), 0) // modes == iota((LANES, LANES), 1) // gw
+
+    def long_carry(i, c):
+        d = lax.rem(me + 1 + i, n)
+        for u in range(per):
+            j = d * per + u
+            at = lanes(j * LANES, LANES)
+            rate, gain = gain_of(j)
+            rate_m = pick(jnp.broadcast_to(column(rate), (LANES, LANES)), modes, lane_group_m)
+            decay = jnp.exp(-rate_m * float(rows))
+            carry = lax.fori_loop(
+                0, me, lambda p, s: s * decay + s_all[p, :, at].astype(f32),
+                jnp.zeros((modes, LANES), f32),
+            )
+            full = jnp.where(same, jnp.concatenate([carry] * gpt, axis=0), 0.0)
+            high = full.astype(bf16)
+            low = (full - high.astype(f32)).astype(bf16)
+            emit = (gain * jnp.exp(-after * rate)).astype(bf16)
+            conv = lc[:, at] + jnp.dot(
+                jnp.concatenate([emit, emit], axis=1),
+                jnp.concatenate([high, low], axis=0),
+                preferred_element_type=f32,
+            )
+            vb[:, at] = (st[:, at].astype(f32) + lq_ref[:, at].astype(f32) * conv).astype(bf16)
+
+        @pl.when(i < n - 1)
+        def _():
+            spread(vb, vh, vss, vrs, d, me).start()
+
+        return c
+
+    lax.fori_loop(0, n, long_carry, 0)
+    own_v = pltpu.make_async_copy(vb.at[:, lanes(me * width, width)], vh.at[block(me), :], own.at[2])
+    own_v.start()
+    own_q.wait()
+    own_k.wait()
+    own_v.wait()
+
+    def arrived(i, c):
+        p = lax.rem(me + n - i, n)
+        spread(q_hbm, qh, qss, qrs, me, p).wait_recv()
+        spread(k_hbm, kh, kss, krs, me, p).wait_recv()
+        spread(vb, vh, vss, vrs, me, p).wait_recv()
+        return c
+
+    lax.fori_loop(1, n, arrived, 0)
+
+    factor = HEAD_DIM ** (-0.5) * 1.4426950408889634
+    below = iota((rows, rows), 1) <= iota((rows, rows), 0)
+
+    def attend(i, c):
+        r = lax.rem(me + 1 + i, n)
+        qs = [qh[block(r), u * LANES : (u + 1) * LANES] for u in range(per)]
+
+        def part(b, state, masked):
+            new = []
+            for u in range(per):
+                peak, total, acc = state[u]
+                cols = slice(u * LANES, (u + 1) * LANES)
+                s = lax.dot_general(
+                    qs[u], kh[block(b), cols], (((1,), (1,)), ((), ())), preferred_element_type=f32
+                ) * factor
+                if masked:
+                    s = jnp.where(below, s, -1e30)
+                top = jnp.maximum(peak, jnp.max(s, axis=1, keepdims=True))
+                w = jnp.exp2(s - top)
+                shrink = jnp.exp2(peak - top)
+                total = total * shrink + jnp.sum(w, axis=1, keepdims=True)
+                acc = acc * shrink + jnp.dot(
+                    w.astype(bf16), vh[block(b), cols], preferred_element_type=f32
+                )
+                new.append((top, total, acc))
+            return tuple(new)
+
+        start = tuple(
+            (jnp.full((rows, 1), -1e30, f32), jnp.zeros((rows, 1), f32), jnp.zeros((rows, LANES), f32))
+            for u in range(per)
+        )
+        state = part(r, start, True)
+        state = lax.fori_loop(0, r, lambda b, s: part(b, s, False), state)
+        for u in range(per):
+            peak, total, acc = state[u]
+            cols = slice(u * LANES, (u + 1) * LANES)
+            got = (acc / total).astype(bf16)
+            ob[block(r), cols] = (vh[block(r), cols].astype(f32) + got.astype(f32)).astype(bf16)
+
+        @pl.when(i < n - 1)
+        def _():
+            give_back(r, me).start()
+
+        return c
+
+    lax.fori_loop(0, n, attend, 0)
+    own_o = pltpu.make_async_copy(ob.at[block(me), :], out_hbm.at[:, lanes(me * width, width)], own.at[3])
+    own_o.start()
+
+    @pl.when(me < n - 1)
+    def _():
+        se_halo.wait_send()
+        mr_halo.wait_send()
+
+    def sent_state(p, c):
+        state_copy(p, me).wait_send()
+        return c
+
+    lax.fori_loop(me + 1, n, sent_state, 0)
+
+    def finish(i, c):
+        p = lax.rem(me + i, n)
+        spread(q_hbm, qh, qss, qrs, p, me).wait_send()
+        spread(k_hbm, kh, kss, krs, p, me).wait_send()
+        spread(vb, vh, vss, vrs, p, me).wait_send()
+        give_back(p, me).wait_send()
+        give_back(me, p).wait_recv()
+        return c
+
+    lax.fori_loop(1, n, finish, 0)
+    own_o.wait()
+
+
+def by_heads(
+    token_ids, embed_table, se_query, se_key, se_filter, mr_query, mr_key, mr_filter,
+    li_query, li_key, li_rate, li_residue, attn_query, attn_key,
+):
+    f32, bf16 = jnp.float32, jnp.bfloat16
+    n = lax.axis_size("seq")
+    rows, chans = se_query.shape
+    groups, mr_taps = mr_filter.shape
+    tiles = chans // LANES
+    width = chans // n
+    group_width = chans // groups
+    modes = li_rate.shape[1]
+    short_taps = jnp.repeat(se_filter.astype(f32).T, group_width, axis=1)
+    reversed_mr = jnp.concatenate(
+        [jnp.zeros((groups, rows - mr_taps), f32), mr_filter.astype(f32)[:, ::-1]], axis=1
+    )
+    vmem = pl.BlockSpec(memory_space=pltpu.VMEM)
+    anywhere = pl.BlockSpec(memory_space=pl.ANY)
+    dma = pltpu.SemaphoreType.DMA
+    return pl.pallas_call(
+        functools.partial(fused, n, n * rows),
+        out_shape=jax.ShapeDtypeStruct((rows, chans), bf16),
+        in_specs=[vmem] * 12 + [anywhere] * 2,
+        out_specs=anywhere,
+        scratch_shapes=[
+            pltpu.VMEM((rows, chans), bf16),
+            pltpu.VMEM((rows + HALO, chans), f32),
+            pltpu.VMEM((HALO, chans), bf16),
+            pltpu.VMEM((HALO, chans), bf16),
+            pltpu.VMEM((rows + rows // 2, chans), bf16),
+            pltpu.VMEM((rows, chans), bf16),
+            pltpu.VMEM((rows, chans), f32),
+            pltpu.VMEM((groups // tiles * rows // 2, rows), bf16),
+            pltpu.VMEM((modes, chans), bf16),
+            pltpu.VMEM((n, modes, chans), bf16),
+            pltpu.VMEM((n * rows, width), bf16),
+            pltpu.VMEM((n * rows, width), bf16),
+            pltpu.VMEM((n * rows, width), bf16),
+            pltpu.VMEM((n * rows, width), bf16),
+            pltpu.VMEM((rows, chans), bf16),
+        ]
+        + [dma((n,))] * 8 + [dma((2,))] * 2 + [dma((n,))] * 2 + [dma((4,))],
+        compiler_params=pltpu.CompilerParams(
+            collective_id=0, has_side_effects=True, vmem_limit_bytes=52 * 2**20
+        ),
+    )(
+        token_ids.astype(f32).reshape(1, rows), embed_table, se_query, se_key, short_taps,
+        mr_query, mr_key, reversed_mr, li_query, li_key,
+        li_rate.reshape(tiles, LANES), li_residue.reshape(tiles, LANES), attn_query, attn_key,
+    )
+
+
+def choose(*args):
+    n = lax.axis_size("seq")
+    rows, chans = args[2].shape
+    groups, mr_taps = args[7].shape
+    modes = args[10].shape[1]
+    fits = (
+        chans % (n * LANES) == 0
+        and HEAD_DIM == LANES
+        and rows == 2 * mr_taps
+        and mr_taps == LANES
+        and chans // groups == modes
+        and modes == HALO
+        and args[4].shape[1] <= HALO
+        and n > 1
+    )
+    return by_heads(*args) if fits else local(*args)
+
+
 def solution(mesh):
     in_specs = (
         P("seq"),
@@ -233,4 +653,4 @@
         P("seq", "chan"),
     )
     out_specs = P("seq", "chan")
-    return jax.shard_map(local, mesh=mesh, in_specs=in_specs, out_specs=out_specs, check_vma=False)
+    return jax.shard_map(choose, mesh=mesh, in_specs=in_specs, out_specs=out_specs, check_vma=False)

time: 417 us -> 163 us (0.39); the launches traced: 411 us -> 161 us
  Pallas kernels: 0 us -> 156 us
  blocking collectives: 150 us -> 0 us
  matrix products: 113 us -> 0 us
  local copies, waits for them, and re-layouts: 53.5 us -> 4.01 us
  waiting for transfers between devices: 31.1 us -> 0 us
  starting transfers between devices: 24.7 us -> 0 us
  other arithmetic: 24.6 us -> 1.36 us
  between operations: 13.8 us -> 0.03 us
    pallas_call x0 -> x1, Pallas kernels: none -> 156 us  [by_heads(): pl.pallas_call(functools.partial(fused, n, n * rows), out_shape=jax.Shape...]
    all_to_all x5 -> x0, blocking collectives: 118 us -> none  [the longest x1 29.1 us: local(): lax.all_to_all(attended, 'seq', split_axis=0, concat_axis=1, tiled=True)]
    dot_general x12 -> x0, matrix products: 93.2 us -> none  [the longest x1 17.5 us: local(): jnp.einsum('bdgm,dmgc->bmgc', mixing, block_states, precision=HIGHEST)]
    all_gather x1 -> x0, blocking collectives: 31.2 us -> none  [carried_in(): everything = jax.tree.map(lambda part: lax.all_gather(part, axis), value)]
    all_to_all x3 -> x0, waiting for transfers between devices: 24.8 us -> none  [the longest x1 24.8 us: local(): lax.all_to_all(lax.all_to_all(queries, 'chan', split_axis=0, concat_axis=...]
    sub x1 -> x0, matrix products: 20 us -> none  [attend_block(): weights = jnp.where(allowed[None], jnp.exp(scores - peak), 0.0)]
    convert_element_type x6 -> x0, local copies, waits for them, and re-layouts: 16.4 us -> none  [the longest x1 6.74 us: local(): current = current_f.astype(bf16)]
    all_to_all x3 -> x0, starting transfers between devices: 14.7 us -> none  [the longest x1 6.71 us: local(): lax.all_to_all(lax.all_to_all(keys_local, 'chan', split_axis=0, concat_ax...]
  transfers between devices with their start and end apart: 8 -> 0, of which waited for: 3 -> 0; matrix products, arithmetic and copies ran while one was open for 41% -> 0% of each run, Pallas kernels for 0% -> 0%
where the time goes in v1:
time: 163 us; the launch traced here: 161 us
  Pallas kernels  156 us (96%)
  local copies, waits for them, and re-layouts  4.01 us (2%)
    pallas_call x1, Pallas kernels, by_heads(): pl.pallas_call(functools.partial(fused, n, n * rows), out_shape=jax.Shape...  156 us

profile of v1, /device:TPU:0, one launch (start us, length us, event | category | flops | bytes accessed | tf_op | source)
XLA Modules:
  0.0 161.3 jit_solution(5874564711436165945)
XLA Ops:
  0.0 0.7 convert_element_type.7
  0.7 0.7 convert_bitcast_fusion
  1.4 0.8 rev.3
  2.2 0.8 copy.17
  3.0 0.1 reshape.14.rate_ref
  3.1 0.8 copy.18
  3.9 0.1 reshape.15.res_ref
  4.0 0.2 broadcast_in_dim.4
  4.2 0.3 reshape.13.sw_ref
  4.4 155.9 %shard_map.136 = bf16[256,2048]{1,0:T(8,128)(2,1)S(1)} custom-call(f32[1,256]{1,0:T(1,128)S(1)} %bitcast.3, bf16[512,2048]{1,0:T(8,128)(2,1)} %table_ref.1, bf16[256,2048]{1,0:T(8,128)(2,1)} %sq_ref.1, bf16[256,2048]{1,0:T(8,128)(2,1)} %sk_ref.1, f32[7,2048]{1,0:T(8,128)S(1)} %reshape.13.sw_ref, bf16[256,2048]{1,0:T(8,128)(2,1)} %mq_ref.1, ...), custom_call_target="tpu_custom_call" | custom-call | tf_op jit(solution)/shard_map/pallas_call | solution.py:587
  160.3 1.0 copy.20
  (1 shorter events, 0.0 us)

commit v2 on v1

--- a/solution.py
+++ b/solution.py
@@ -227,7 +227,7 @@
     n, total_len,
     ids_ref, table_ref, sq_ref, sk_ref, sw_ref, mq_ref, mk_ref, mf_ref, lq_ref, lk_ref,
     rate_ref, res_ref, q_hbm, k_hbm, out_hbm,
-    st, xs, hs, hx, mx, lx, lc, wt, s_mine, s_all, qh, kh, vh, ob, vb,
+    st, xs, hs, hx, mx, lx, lc, wt, s_mine, s_all, qh, kh, vh, ob, vb, sc, pw, tot,
     qss, qrs, kss, krs, vss, vrs, oss, ors, hss, hrs, sss, srs, own,
 ):
     f32, bf16 = jnp.float32, jnp.bfloat16
@@ -358,7 +358,6 @@
     def _():
         mr_halo.start()
 
-    send_all(k_hbm, kh, kss, krs)
 
     @pl.when(me > 0)
     def _():
@@ -422,6 +421,7 @@
         return c
 
     lax.fori_loop(me + 1, n, push_state, 0)
+    send_all(k_hbm, kh, kss, krs)
 
     def long_local(j, c):
         at = lanes(j * LANES, LANES)
@@ -481,55 +481,81 @@
     own_v.start()
     own_q.wait()
     own_k.wait()
-    own_v.wait()
 
     def arrived(i, c):
         p = lax.rem(me + n - i, n)
         spread(q_hbm, qh, qss, qrs, me, p).wait_recv()
         spread(k_hbm, kh, kss, krs, me, p).wait_recv()
-        spread(vb, vh, vss, vrs, me, p).wait_recv()
         return c
 
     lax.fori_loop(1, n, arrived, 0)
 
     factor = HEAD_DIM ** (-0.5) * 1.4426950408889634
     below = iota((rows, rows), 1) <= iota((rows, rows), 0)
-
-    def attend(i, c):
+    heads = [slice(u * LANES, (u + 1) * LANES) for u in range(per)]
+
+    def weigh(i, c):
         r = lax.rem(me + 1 + i, n)
-        qs = [qh[block(r), u * LANES : (u + 1) * LANES] for u in range(per)]
-
-        def part(b, state, masked):
+        qs = [qh[block(r), cols] for cols in heads]
+
+        def score(b, tops, masked):
             new = []
             for u in range(per):
-                peak, total, acc = state[u]
-                cols = slice(u * LANES, (u + 1) * LANES)
                 s = lax.dot_general(
-                    qs[u], kh[block(b), cols], (((1,), (1,)), ((), ())), preferred_element_type=f32
+                    qs[u], kh[block(b), heads[u]], (((1,), (1,)), ((), ())),
+                    preferred_element_type=f32,
                 ) * factor
                 if masked:
                     s = jnp.where(below, s, -1e30)
-                top = jnp.maximum(peak, jnp.max(s, axis=1, keepdims=True))
-                w = jnp.exp2(s - top)
-                shrink = jnp.exp2(peak - top)
-                total = total * shrink + jnp.sum(w, axis=1, keepdims=True)
-                acc = acc * shrink + jnp.dot(
-                    w.astype(bf16), vh[block(b), cols], preferred_element_type=f32
+                sc[u, :, block(b)] = s
+                new.append(jnp.maximum(tops[u], jnp.maximum(s[:, :LANES], s[:, LANES:])))
+            return tuple(new)
+
+        tops = score(r, (jnp.full((rows, LANES), -1e30, f32),) * per, True)
+        tops = lax.fori_loop(0, r, lambda b, t: score(b, t, False), tops)
+        peaks = [jnp.max(t, axis=1, keepdims=True) for t in tops]
+
+        def weight(b, sums):
+            new = []
+            for u in range(per):
+                w = jnp.exp2(sc[u, :, block(b)] - peaks[u])
+                pw[u, block(r), block(b)] = w.astype(bf16)
+                new.append(sums[u] + (w[:, :LANES] + w[:, LANES:]))
+            return tuple(new)
+
+        sums = lax.fori_loop(0, r + 1, weight, (jnp.zeros((rows, LANES), f32),) * per)
+        for u in range(per):
+            tot[u, block(r), :] = jnp.broadcast_to(
+                jnp.sum(sums[u], axis=1, keepdims=True), (rows, LANES)
+            )
+        return c
+
+    lax.fori_loop(0, n, weigh, 0)
+    own_v.wait()
+
+    def values_in(i, c):
+        spread(vb, vh, vss, vrs, me, lax.rem(me + n - i, n)).wait_recv()
+        return c
+
+    lax.fori_loop(1, n, values_in, 0)
+
+    def attend(i, c):
+        r = lax.rem(me + 1 + i, n)
+
+        def mix(b, accs):
+            return tuple(
+                accs[u] + jnp.dot(
+                    pw[u, block(r), block(b)], vh[block(b), heads[u]], preferred_element_type=f32
                 )
-                new.append((top, total, acc))
-            return tuple(new)
-
-        start = tuple(
-            (jnp.full((rows, 1), -1e30, f32), jnp.zeros((rows, 1), f32), jnp.zeros((rows, LANES), f32))
-            for u in range(per)
-        )
-        state = part(r, start, True)
-        state = lax.fori_loop(0, r, lambda b, s: part(b, s, False), state)
+                for u in range(per)
+            )
+
+        accs = lax.fori_loop(0, r + 1, mix, (jnp.zeros((rows, LANES), f32),) * per)
         for u in range(per):
-            peak, total, acc = state[u]
-            cols = slice(u * LANES, (u + 1) * LANES)
-            got = (acc / total).astype(bf16)
-            ob[block(r), cols] = (vh[block(r), cols].astype(f32) + got.astype(f32)).astype(bf16)
+            got = (accs[u] / tot[u, block(r), :]).astype(bf16)
+            ob[block(r), heads[u]] = (
+                vh[block(r), heads[u]].astype(f32) + got.astype(f32)
+            ).astype(bf16)
 
         @pl.when(i < n - 1)
         def _():
@@ -605,10 +631,13 @@
             pltpu.VMEM((n * rows, width), bf16),
             pltpu.VMEM((n * rows, width), bf16),
             pltpu.VMEM((rows, chans), bf16),
+            pltpu.VMEM((width // LANES, rows, n * rows), f32),
+            pltpu.VMEM((width // LANES, n * rows, n * rows), bf16),
+            pltpu.VMEM((width // LANES, n * rows, LANES), f32),
         ]
         + [dma((n,))] * 8 + [dma((2,))] * 2 + [dma((n,))] * 2 + [dma((4,))],
         compiler_params=pltpu.CompilerParams(
-            collective_id=0, has_side_effects=True, vmem_limit_bytes=52 * 2**20
+            collective_id=0, has_side_effects=True, vmem_limit_bytes=58 * 2**20
         ),
     )(
         token_ids.astype(f32).reshape(1, rows), embed_table, se_query, se_key, short_taps,

time: 163 us -> 144 us (0.88)
  the two profiles are of different devices: /device:TPU:0 before, /device:TPU:18 now
where the time goes in v2:
time: 144 us; the launch traced here: 143 us
  Pallas kernels  133 us (92%)
  local copies, waits for them, and re-layouts  7.81 us (5%)
  other arithmetic  1.93 us (1%)
    pallas_call x1, Pallas kernels, by_heads(): pl.pallas_call(functools.partial(fused, n, n * rows), out_shape=jax.Shape...  133 us
    unnamed x3, local copies, waits for them, and re-layouts  3.89 us

profile of v2, /device:TPU:18, one launch (start us, length us, event | category | flops | bytes accessed | tf_op | source)
XLA Modules:
  0.0 143.2 jit_solution(12791342202343997204)
XLA Ops:
  0.0 1.3 convert_element_type.7
  1.3 0.7 convert_bitcast_fusion
  1.9 0.8 rev.3
  2.8 0.7 concatenate.3.mf_ref
  3.4 0.8 copy.17
  4.2 0.7 reshape.14.rate_ref
  4.9 0.8 copy.18
  5.7 0.7 reshape.15.res_ref
  6.4 0.2 broadcast_in_dim.4
  6.6 0.9 reshape.13.sw_ref
  7.5 133.4 %shard_map.136 = bf16[256,2048]{1,0:T(8,128)(2,1)} custom-call(f32[1,256]{1,0:T(1,128)} %bitcast.3, bf16[512,2048]{1,0:T(8,128)(2,1)} %table_ref.1, bf16[256,2048]{1,0:T(8,128)(2,1)} %sq_ref.1, bf16[256,2048]{1,0:T(8,128)(2,1)} %sk_ref.1, f32[7,2048]{1,0:T(8,128)} %reshape.13.sw_ref, bf16[256,2048]{1,0:T(8,128)(2,1)} %mq_ref.1, bf16[256,2048]{1,0:T(8,128)(2,1)} %mk_ref.1, ...), custom_call_target="tpu_custom_call" | custom-call | tf_op jit(solution)/shard_map/pallas_call | solution.py:613
  140.9 2.3 %copy.20 = bf16[256,2048]{1,0:T(8,128)(2,1)} copy(bf16[256,2048]{1,0:T(8,128)(2,1)} %shard_map.136) | data formatting | bytes 2097152

commit v3 on v2

--- a/solution.py
+++ b/solution.py
@@ -534,13 +534,17 @@
     own_v.wait()
 
     def values_in(i, c):
-        spread(vb, vh, vss, vrs, me, lax.rem(me + n - i, n)).wait_recv()
-        return c
-
-    lax.fori_loop(1, n, values_in, 0)
+        spread(vb, vh, vss, vrs, me, i).wait_recv()
+        return c
+
+    lax.fori_loop(0, me, values_in, 0)
 
     def attend(i, c):
-        r = lax.rem(me + 1 + i, n)
+        r = lax.rem(me + 2 * n - 1 - i, n)
+
+        @pl.when(i == me)
+        def _():
+            lax.fori_loop(me + 1, n, values_in, 0)
 
         def mix(b, accs):
             return tuple(

time: 144 us -> 151 us (1.049)
  the two profiles are of different devices: /device:TPU:18 before, /device:TPU:0 now
where the time goes in v3:
time: 151 us; the launch traced here: 150 us
  Pallas kernels  141 us (93%)
  local copies, waits for them, and re-layouts  7.81 us (5%)
  other arithmetic  1.93 us (1%)
    pallas_call x1, Pallas kernels, by_heads(): pl.pallas_call(functools.partial(fused, n, n * rows), out_shape=jax.Shape...  141 us
    unnamed x3, local copies, waits for them, and re-layouts  3.89 us

profile of v3, /device:TPU:0, one launch (start us, length us, event | category | flops | bytes accessed | tf_op | source)
XLA Modules:
  0.0 150.3 jit_solution(12783267494832815462)
XLA Ops:
  0.0 1.3 convert_element_type.7
  1.3 0.7 convert_bitcast_fusion
  1.9 0.8 rev.3
  2.8 0.7 concatenate.3.mf_ref
  3.4 0.8 copy.17
  4.2 0.7 reshape.14.rate_ref
  4.9 0.8 copy.18
  5.7 0.7 reshape.15.res_ref
  6.4 0.2 broadcast_in_dim.4
  6.6 0.9 reshape.13.sw_ref
  7.5 140.5 %shard_map.136 = bf16[256,2048]{1,0:T(8,128)(2,1)} custom-call(f32[1,256]{1,0:T(1,128)} %bitcast.3, bf16[512,2048]{1,0:T(8,128)(2,1)} %table_ref.1, bf16[256,2048]{1,0:T(8,128)(2,1)} %sq_ref.1, bf16[256,2048]{1,0:T(8,128)(2,1)} %sk_ref.1, f32[7,2048]{1,0:T(8,128)} %reshape.13.sw_ref, bf16[256,2048]{1,0:T(8,128)(2,1)} %mq_ref.1, bf16[256,2048]{1,0:T(8,128)(2,1)} %mk_ref.1, ...), custom_call_target="tpu_custom_call" | custom-call | tf_op jit(solution)/shard_map/pallas_call | solution.py:617
  148.0 2.3 %copy.20 = bf16[256,2048]{1,0:T(8,128)(2,1)} copy(bf16[256,2048]{1,0:T(8,128)(2,1)} %shard_map.136) | data formatting | bytes 2097152
